TPU v7x, 256 devices: a whole 4x4x8 slice. The times are simulated.
256 devices in a mesh: ctx: 64 (over x_lo, z, y), tp: 4 (over x_hi, core).
Axes of the slice: x: 4 (x_hi: 2, x_lo: 2; x = x_hi * 2 + x_lo), y: 4, z: 8, core: 2. Of those that a mesh axis runs over, the one named last changes fastest.
Arguments:
- queries: bfloat16 [8192, 4096], P('ctx', 'tp'), may hold values from -9 to 9
- key_rows: bfloat16 [8192, 512], P('ctx', 'tp'), may hold values from -6 to 6
- value_rows: bfloat16 [8192, 512], P('ctx', 'tp'), may hold values from -6 to 6
- attn_out: bfloat16 [8192, 4096], P('ctx', 'tp'), may hold values from -1.5 to 1.5
- log_norm: float32 [8192, 32], P('ctx', 'tp'), as said below
- grad_out: bfloat16 [8192, 4096], P(('ctx', 'tp')), may hold values from -6 to 6
- block_pos: int32 [128], replicated, may hold values from 0 to 127, as said below
Outputs:
- query_grad: bfloat16 [8192, 4096], P(('ctx', 'tp'))
- key_grad: bfloat16 [8192, 512], P(('ctx', 'tp'))
- value_grad: bfloat16 [8192, 512], P(('ctx', 'tp'))
Inputs may be any that keep to these rules, and one draw needn't show every extreme that they name: `block_pos`: a permutation of 0 to 127. log_norm[i, h] lies between 0.8 and 1.6 above the natural logarithm of pos[i] + 1.
All inputs are finite; a program needn't handle non-finite values.
Results may differ from a plain program's by a relative error of at most 0.005.
Values may be sent and summed in bfloat16 or wider, within the bound.
A program may use at most 64 MiB of HBM per device.

v0:
```python
import jax
import jax.numpy as jnp
from jax import lax
from jax.sharding import PartitionSpec as P

HEADS = 32
KV_HEADS = 4
HEAD_DIM = 128


def from_behind(value, axis, steps):
    count = lax.axis_size(axis)
    pairs = [(source, (source + steps) % count) for source in range(count)]
    return lax.ppermute(value, axis, pairs)


def attend(query_heads, grad_heads, deltas, norm_heads, query_pos, key_pair, key_pos):
    key_len = key_pair.shape[1]
    kv_local = query_heads.shape[1]
    key_heads = key_pair[0].reshape(key_len, kv_local, HEAD_DIM)
    value_heads = key_pair[1].reshape(key_len, kv_local, HEAD_DIM)
    scores = jnp.einsum(
        "rkgd,nkd->kgrn", query_heads, key_heads, preferred_element_type=jnp.float32
    ) * HEAD_DIM ** (-0.5)
    allowed = query_pos[:, None] >= key_pos[None, :]
    attn_prob = jnp.where(allowed, jnp.exp(scores - norm_heads[..., None]), 0.0)
    prob_grad = jnp.einsum(
        "rkgd,nkd->kgrn", grad_heads, value_heads, preferred_element_type=jnp.float32
    )
    score_grad = (attn_prob * (prob_grad - deltas[..., None])).astype(jnp.bfloat16)
    value_add = jnp.einsum(
        "kgrn,rkgd->nkd",
        attn_prob.astype(jnp.bfloat16),
        grad_heads,
        preferred_element_type=jnp.float32,
    )
    key_add = jnp.einsum(
        "kgrn,rkgd->nkd", score_grad, query_heads, preferred_element_type=jnp.float32
    )
    query_add = jnp.einsum(
        "kgrn,nkd->rkgd", score_grad, key_heads, preferred_element_type=jnp.float32
    )
    return (query_add, jnp.stack([key_add.reshape(key_len, -1), value_add.reshape(key_len, -1)]))


def pass_keys(key_pair):
    return from_behind(key_pair, "ctx", 1)


def pass_grads(pair_grad):
    return from_behind(pair_grad, "ctx", 1)


def per_device(queries, key_rows, value_rows, attn_out, log_norm, grad_out, block_pos):
    cycle_len = lax.axis_size("ctx")
    cycle_idx = lax.axis_index("ctx")
    local_rows = queries.shape[0]
    half_rows = local_rows // 2
    group_size = HEADS // KV_HEADS
    kv_local = key_rows.shape[1] // HEAD_DIM
    scaling = HEAD_DIM ** (-0.5)
    grad_local = lax.all_to_all(grad_out, "tp", split_axis=1, concat_axis=0, tiled=True)
    query_heads = queries.reshape(local_rows, kv_local, group_size, HEAD_DIM)
    grad_heads = grad_local.reshape(local_rows, kv_local, group_size, HEAD_DIM)
    out_heads = attn_out.reshape(local_rows, kv_local, group_size, HEAD_DIM)
    deltas = jnp.sum(
        grad_heads.astype(jnp.float32) * out_heads.astype(jnp.float32), axis=-1
    ).transpose(1, 2, 0)
    norm_heads = log_norm.reshape(local_rows, kv_local, group_size).transpose(1, 2, 0)
    offsets = jnp.arange(half_rows, dtype=jnp.int32)
    positions = (block_pos[:, None] * half_rows + offsets[None, :]).reshape(-1)
    query_pos = lax.dynamic_slice_in_dim(positions, cycle_idx * local_rows, local_rows)
    key_pair = jnp.stack([key_rows, value_rows])
    query_zero = jnp.zeros((local_rows, kv_local, group_size, HEAD_DIM), jnp.float32)

    def block_terms(visiting, key_pos):
        return attend(query_heads, grad_heads, deltas, norm_heads, query_pos, visiting, key_pos)

    def one_block(turn_idx, visiting):
        source = (cycle_idx - turn_idx) % cycle_len
        key_pos = lax.dynamic_slice_in_dim(positions, source * local_rows, local_rows)
        return block_terms(visiting, key_pos)

    def turn_one(turn_idx, carried):
        visiting, pair_grad, query_grad = carried
        query_add, pair_add = one_block(turn_idx, visiting)
        return (pass_keys(visiting), pass_grads(pair_grad + pair_add), query_grad + query_add)

    pair_zero = jnp.zeros((2, local_rows, kv_local * HEAD_DIM), jnp.float32)
    visiting, pair_grad, query_grad = lax.fori_loop(
        0, cycle_len - 1, turn_one, (key_pair, pair_zero, query_zero)
    )
    query_add, pair_add = one_block(cycle_len - 1, visiting)
    pair_grad = pass_grads(pair_grad + pair_add)
    query_grad = query_grad + query_add
    query_out = (query_grad * scaling).reshape(local_rows, -1).astype(jnp.bfloat16)
    key_out = (pair_grad[0] * scaling).astype(jnp.bfloat16)
    value_out = pair_grad[1].astype(jnp.bfloat16)
    query_tok, key_tok, value_tok = (
        lax.all_to_all(query_out, "tp", split_axis=0, concat_axis=1, tiled=True),
        lax.all_to_all(key_out, "tp", split_axis=0, concat_axis=1, tiled=True),
        lax.all_to_all(value_out, "tp", split_axis=0, concat_axis=1, tiled=True),
    )
    return (query_tok, key_tok, value_tok)


def solution(mesh):
    in_specs = (
        P("ctx", "tp"),
        P("ctx", "tp"),
        P("ctx", "tp"),
        P("ctx", "tp"),
        P("ctx", "tp"),
        P(("ctx", "tp"), None),
        P(),
    )
    out_specs = (P(("ctx", "tp"), None), P(("ctx", "tp"), None), P(("ctx", "tp"), None))
    return jax.shard_map(
        per_device, mesh=mesh, in_specs=in_specs, out_specs=out_specs, check_vma=False
    )
```

profile of v0, /device:TPU:1, one launch (start us, length us, event | category | flops | bytes accessed | tf_op | source)
XLA Modules:
  0.0 739.5 jit_solution(7889496474317784582)
XLA Ops:
  2.3 6.7 all-to-all-start
  16.9 630.2 %while.20 = (s32[]{:T(128)}, bf16[2,128,128]{2,1,0:T(8,128)(2,1)S(1)}, f32[2,128,128]{2,1,0:T(8,128)S(1)}, f32[128,1,8,128]{3,0,2,1:T(8,128)S(1)}, s32[128]{0:T(...) while((s32[]{:T(128)}, ...), condition=%wide.region_2.3_spmd.clone, body=%wide.region_1.2_spmd.clone.sunk | while | flops 169033744 | bytes 6039970 | solution.py:90
  72.9 5.7 collective-permute-done
  91.8 5.7 collective-permute-done
  101.1 5.7 collective-permute-done
  119.7 5.9 collective-permute-done
  129.0 6.7 collective-permute-done
  139.2 6.3 collective-permute-done
  249.7 6.0 collective-permute-done
  259.0 6.5 collective-permute-done
  269.2 6.2 collective-permute-done
  378.6 6.7 collective-permute-done
  388.3 6.7 collective-permute-done
  399.4 5.7 collective-permute-done
  499.2 5.8 collective-permute-done
  508.5 6.7 collective-permute-done
  518.5 6.5 collective-permute-done
  561.9 5.7 collective-permute-done
  572.2 5.7 collective-permute-done
  629.3 5.8 collective-permute-done
  638.6 6.7 collective-permute-done
  649.6 8.2 %collective-permute-done.2 = f32[2,128,128]{2,1,0:T(8,128)S(1)} collective-permute-done((f32[2,128,128]{2,1,0:T(8,128)S(1)}, f32[2,128,128]{2,1,0:T(8,128)S(1)}, u32[]{:S(2)}, u32[]{:S(2)}) %collective-permute-start.2) | collective-permute-done | bytes 131104 | tf_op jit(solution)/shard_map/ppermute | solution.py:14
  658.4 56.2 %all-to-all-start.3 = ((bf16[4,32,128]{2,1,0:T(8,128)(2,1)}), bf16[4,32,128]{2,1,0:T(8,128)(2,1)S(1)}, u32[]{:S(2)}, u32[]{:S(2)}) async-start(bf16[4,32,128]{2,1,0:T(8,128)(2,1)} %bitcast.39), calls=%async_computation.3 | async-start | bytes 65536 | tf_op jit(solution)/shard_map/all_to_all | solution.py:102
  732.7 6.1 all-to-all-done.1
  (850 shorter events, 538.4 us)
Async XLA Ops:
  2.3 13.4 %all-to-all-start = ((bf16[32,4,1024]{2,0,1:T(8,128)(2,1)}), bf16[32,4,1024]{2,0,1:T(8,128)(2,1)S(1)}, u32[]{:S(2)}, u32[]{:S(2)}) async-start(bf16[32,4,1024]{2,0,1:T(8,128)(2,1)} %bitcast.210), calls=%async_computation | async-start | bytes 524288 | tf_op jit(solution)/shard_map/all_to_all | solution.py:62
  18.5 10.8 %collective-permute-start.1 = (f32[2,128,128]{2,1,0:T(8,128)S(1)}, f32[2,128,128]{2,1,0:T(8,128)S(1)}, u32[]{:S(2)}, u32[]{:S(2)}) collective-permute-start(f32[2,128,128]{2,1,0:T(8,128)S(1)} %maximum_add_fusion.3), channel_id=1, source_target_pairs={{0,4},{4,8},{8,12},{12,16},{16,20},{20,24},{24,28},{28,32},{32,36}... | collective-permute-start | bytes 393224 | tf_op jit(solution)/shard_map/while/body/eval_jaxpr/ppermute | solution.py:14
  30.5 9.6 %collective-permute-start.1 = (f32[2,128,128]{2,1,0:T(8,128)S(1)}, f32[2,128,128]{2,1,0:T(8,128)S(1)}, u32[]{:S(2)}, u32[]{:S(2)}) collective-permute-start(f32[2,128,128]{2,1,0:T(8,128)S(1)} %maximum_add_fusion.3), channel_id=1, source_target_pairs={{0,4},{4,8},{8,12},{12,16},{16,20},{20,24},{24,28},{28,32},{32,36}... | collective-permute-start | bytes 393224 | tf_op jit(solution)/shard_map/while/body/eval_jaxpr/ppermute | solution.py:14
  41.4 9.4 %collective-permute-start.1 = (f32[2,128,128]{2,1,0:T(8,128)S(1)}, f32[2,128,128]{2,1,0:T(8,128)S(1)}, u32[]{:S(2)}, u32[]{:S(2)}) collective-permute-start(f32[2,128,128]{2,1,0:T(8,128)S(1)} %maximum_add_fusion.3), channel_id=1, source_target_pairs={{0,4},{4,8},{8,12},{12,16},{16,20},{20,24},{24,28},{28,32},{32,36}... | collective-permute-start | bytes 393224 | tf_op jit(solution)/shard_map/while/body/eval_jaxpr/ppermute | solution.py:14
  138.8 9.6 %collective-permute-start.1 = (f32[2,128,128]{2,1,0:T(8,128)S(1)}, f32[2,128,128]{2,1,0:T(8,128)S(1)}, u32[]{:S(2)}, u32[]{:S(2)}) collective-permute-start(f32[2,128,128]{2,1,0:T(8,128)S(1)} %maximum_add_fusion.3), channel_id=1, source_target_pairs={{0,4},{4,8},{8,12},{12,16},{16,20},{20,24},{24,28},{28,32},{32,36}... | collective-permute-start | bytes 393224 | tf_op jit(solution)/shard_map/while/body/eval_jaxpr/ppermute | solution.py:14
  149.6 9.8 %collective-permute-start.1 = (f32[2,128,128]{2,1,0:T(8,128)S(1)}, f32[2,128,128]{2,1,0:T(8,128)S(1)}, u32[]{:S(2)}, u32[]{:S(2)}) collective-permute-start(f32[2,128,128]{2,1,0:T(8,128)S(1)} %maximum_add_fusion.3), channel_id=1, source_target_pairs={{0,4},{4,8},{8,12},{12,16},{16,20},{20,24},{24,28},{28,32},{32,36}... | collective-permute-start | bytes 393224 | tf_op jit(solution)/shard_map/while/body/eval_jaxpr/ppermute | solution.py:14
  160.6 9.6 %collective-permute-start.1 = (f32[2,128,128]{2,1,0:T(8,128)S(1)}, f32[2,128,128]{2,1,0:T(8,128)S(1)}, u32[]{:S(2)}, u32[]{:S(2)}) collective-permute-start(f32[2,128,128]{2,1,0:T(8,128)S(1)} %maximum_add_fusion.3), channel_id=1, source_target_pairs={{0,4},{4,8},{8,12},{12,16},{16,20},{20,24},{24,28},{28,32},{32,36}... | collective-permute-start | bytes 393224 | tf_op jit(solution)/shard_map/while/body/eval_jaxpr/ppermute | solution.py:14
  171.5 9.4 %collective-permute-start.1 = (f32[2,128,128]{2,1,0:T(8,128)S(1)}, f32[2,128,128]{2,1,0:T(8,128)S(1)}, u32[]{:S(2)}, u32[]{:S(2)}) collective-permute-start(f32[2,128,128]{2,1,0:T(8,128)S(1)} %maximum_add_fusion.3), channel_id=1, source_target_pairs={{0,4},{4,8},{8,12},{12,16},{16,20},{20,24},{24,28},{28,32},{32,36}... | collective-permute-start | bytes 393224 | tf_op jit(solution)/shard_map/while/body/eval_jaxpr/ppermute | solution.py:14
  268.8 9.5 %collective-permute-start.1 = (f32[2,128,128]{2,1,0:T(8,128)S(1)}, f32[2,128,128]{2,1,0:T(8,128)S(1)}, u32[]{:S(2)}, u32[]{:S(2)}) collective-permute-start(f32[2,128,128]{2,1,0:T(8,128)S(1)} %maximum_add_fusion.3), channel_id=1, source_target_pairs={{0,4},{4,8},{8,12},{12,16},{16,20},{20,24},{24,28},{28,32},{32,36}... | collective-permute-start | bytes 393224 | tf_op jit(solution)/shard_map/while/body/eval_jaxpr/ppermute | solution.py:14
  279.5 9.8 %collective-permute-start.1 = (f32[2,128,128]{2,1,0:T(8,128)S(1)}, f32[2,128,128]{2,1,0:T(8,128)S(1)}, u32[]{:S(2)}, u32[]{:S(2)}) collective-permute-start(f32[2,128,128]{2,1,0:T(8,128)S(1)} %maximum_add_fusion.3), channel_id=1, source_target_pairs={{0,4},{4,8},{8,12},{12,16},{16,20},{20,24},{24,28},{28,32},{32,36}... | collective-permute-start | bytes 393224 | tf_op jit(solution)/shard_map/while/body/eval_jaxpr/ppermute | solution.py:14
  290.5 9.5 %collective-permute-start.1 = (f32[2,128,128]{2,1,0:T(8,128)S(1)}, f32[2,128,128]{2,1,0:T(8,128)S(1)}, u32[]{:S(2)}, u32[]{:S(2)}) collective-permute-start(f32[2,128,128]{2,1,0:T(8,128)S(1)} %maximum_add_fusion.3), channel_id=1, source_target_pairs={{0,4},{4,8},{8,12},{12,16},{16,20},{20,24},{24,28},{28,32},{32,36}... | collective-permute-start | bytes 393224 | tf_op jit(solution)/shard_map/while/body/eval_jaxpr/ppermute | solution.py:14
  301.2 9.3 %collective-permute-start.1 = (f32[2,128,128]{2,1,0:T(8,128)S(1)}, f32[2,128,128]{2,1,0:T(8,128)S(1)}, u32[]{:S(2)}, u32[]{:S(2)}) collective-permute-start(f32[2,128,128]{2,1,0:T(8,128)S(1)} %maximum_add_fusion.3), channel_id=1, source_target_pairs={{0,4},{4,8},{8,12},{12,16},{16,20},{20,24},{24,28},{28,32},{32,36}... | collective-permute-start | bytes 393224 | tf_op jit(solution)/shard_map/while/body/eval_jaxpr/ppermute | solution.py:14
  387.9 9.9 %collective-permute-start.1 = (f32[2,128,128]{2,1,0:T(8,128)S(1)}, f32[2,128,128]{2,1,0:T(8,128)S(1)}, u32[]{:S(2)}, u32[]{:S(2)}) collective-permute-start(f32[2,128,128]{2,1,0:T(8,128)S(1)} %maximum_add_fusion.3), channel_id=1, source_target_pairs={{0,4},{4,8},{8,12},{12,16},{16,20},{20,24},{24,28},{28,32},{32,36}... | collective-permute-start | bytes 393224 | tf_op jit(solution)/shard_map/while/body/eval_jaxpr/ppermute | solution.py:14
  399.0 9.6 %collective-permute-start.1 = (f32[2,128,128]{2,1,0:T(8,128)S(1)}, f32[2,128,128]{2,1,0:T(8,128)S(1)}, u32[]{:S(2)}, u32[]{:S(2)}) collective-permute-start(f32[2,128,128]{2,1,0:T(8,128)S(1)} %maximum_add_fusion.3), channel_id=1, source_target_pairs={{0,4},{4,8},{8,12},{12,16},{16,20},{20,24},{24,28},{28,32},{32,36}... | collective-permute-start | bytes 393224 | tf_op jit(solution)/shard_map/while/body/eval_jaxpr/ppermute | solution.py:14
  409.8 9.7 %collective-permute-start.1 = (f32[2,128,128]{2,1,0:T(8,128)S(1)}, f32[2,128,128]{2,1,0:T(8,128)S(1)}, u32[]{:S(2)}, u32[]{:S(2)}) collective-permute-start(f32[2,128,128]{2,1,0:T(8,128)S(1)} %maximum_add_fusion.3), channel_id=1, source_target_pairs={{0,4},{4,8},{8,12},{12,16},{16,20},{20,24},{24,28},{28,32},{32,36}... | collective-permute-start | bytes 393224 | tf_op jit(solution)/shard_map/while/body/eval_jaxpr/ppermute | solution.py:14
  420.7 9.5 %collective-permute-start.1 = (f32[2,128,128]{2,1,0:T(8,128)S(1)}, f32[2,128,128]{2,1,0:T(8,128)S(1)}, u32[]{:S(2)}, u32[]{:S(2)}) collective-permute-start(f32[2,128,128]{2,1,0:T(8,128)S(1)} %maximum_add_fusion.3), channel_id=1, source_target_pairs={{0,4},{4,8},{8,12},{12,16},{16,20},{20,24},{24,28},{28,32},{32,36}... | collective-permute-start | bytes 393224 | tf_op jit(solution)/shard_map/while/body/eval_jaxpr/ppermute | solution.py:14
  431.3 9.2 %collective-permute-start.1 = (f32[2,128,128]{2,1,0:T(8,128)S(1)}, f32[2,128,128]{2,1,0:T(8,128)S(1)}, u32[]{:S(2)}, u32[]{:S(2)}) collective-permute-start(f32[2,128,128]{2,1,0:T(8,128)S(1)} %maximum_add_fusion.3), channel_id=1, source_target_pairs={{0,4},{4,8},{8,12},{12,16},{16,20},{20,24},{24,28},{28,32},{32,36}... | collective-permute-start | bytes 393224 | tf_op jit(solution)/shard_map/while/body/eval_jaxpr/ppermute | solution.py:14
  518.1 9.8 %collective-permute-start.1 = (f32[2,128,128]{2,1,0:T(8,128)S(1)}, f32[2,128,128]{2,1,0:T(8,128)S(1)}, u32[]{:S(2)}, u32[]{:S(2)}) collective-permute-start(f32[2,128,128]{2,1,0:T(8,128)S(1)} %maximum_add_fusion.3), channel_id=1, source_target_pairs={{0,4},{4,8},{8,12},{12,16},{16,20},{20,24},{24,28},{28,32},{32,36}... | collective-permute-start | bytes 393224 | tf_op jit(solution)/shard_map/while/body/eval_jaxpr/ppermute | solution.py:14
  529.1 9.7 %collective-permute-start.1 = (f32[2,128,128]{2,1,0:T(8,128)S(1)}, f32[2,128,128]{2,1,0:T(8,128)S(1)}, u32[]{:S(2)}, u32[]{:S(2)}) collective-permute-start(f32[2,128,128]{2,1,0:T(8,128)S(1)} %maximum_add_fusion.3), channel_id=1, source_target_pairs={{0,4},{4,8},{8,12},{12,16},{16,20},{20,24},{24,28},{28,32},{32,36}... | collective-permute-start | bytes 393224 | tf_op jit(solution)/shard_map/while/body/eval_jaxpr/ppermute | solution.py:14
  540.0 9.7 %collective-permute-start.1 = (f32[2,128,128]{2,1,0:T(8,128)S(1)}, f32[2,128,128]{2,1,0:T(8,128)S(1)}, u32[]{:S(2)}, u32[]{:S(2)}) collective-permute-start(f32[2,128,128]{2,1,0:T(8,128)S(1)} %maximum_add_fusion.3), channel_id=1, source_target_pairs={{0,4},{4,8},{8,12},{12,16},{16,20},{20,24},{24,28},{28,32},{32,36}... | collective-permute-start | bytes 393224 | tf_op jit(solution)/shard_map/while/body/eval_jaxpr/ppermute | solution.py:14
  550.8 9.4 %collective-permute-start.1 = (f32[2,128,128]{2,1,0:T(8,128)S(1)}, f32[2,128,128]{2,1,0:T(8,128)S(1)}, u32[]{:S(2)}, u32[]{:S(2)}) collective-permute-start(f32[2,128,128]{2,1,0:T(8,128)S(1)} %maximum_add_fusion.3), channel_id=1, source_target_pairs={{0,4},{4,8},{8,12},{12,16},{16,20},{20,24},{24,28},{28,32},{32,36}... | collective-permute-start | bytes 393224 | tf_op jit(solution)/shard_map/while/body/eval_jaxpr/ppermute | solution.py:14
  648.2 9.6 %collective-permute-start.2 = (f32[2,128,128]{2,1,0:T(8,128)S(1)}, f32[2,128,128]{2,1,0:T(8,128)S(1)}, u32[]{:S(2)}, u32[]{:S(2)}) collective-permute-start(f32[2,128,128]{2,1,0:T(8,128)S(1)} %maximum_add_fusion.1), channel_id=1, source_target_pairs={{0,4},{4,8},{8,12},{12,16},{16,20},{20,24},{24,28},{28,32},{32,36}... | collective-permute-start | bytes 393224 | tf_op jit(solution)/shard_map/ppermute | solution.py:14
  658.4 60.9 %all-to-all-start.3 = ((bf16[4,32,128]{2,1,0:T(8,128)(2,1)}), bf16[4,32,128]{2,1,0:T(8,128)(2,1)S(1)}, u32[]{:S(2)}, u32[]{:S(2)}) async-start(bf16[4,32,128]{2,1,0:T(8,128)(2,1)} %bitcast.39), calls=%async_computation.3 | async-start | bytes 65536 | tf_op jit(solution)/shard_map/all_to_all | solution.py:102
  728.0 10.8 %all-to-all-start.1 = ((bf16[4,32,1024]{2,1,0:T(8,128)(2,1)}), bf16[4,32,1024]{2,1,0:T(8,128)(2,1)S(1)}, u32[]{:S(2)}, u32[]{:S(2)}) async-start(bf16[4,32,1024]{2,1,0:T(8,128)(2,1)} %convert_element_type.75), calls=%async_computation.1 | async-start | bytes 524288 | tf_op jit(solution)/shard_map/all_to_all | solution.py:100
  (113 other events, 853.3 us)
where the time goes:
time: 740 us; the launch traced here: 739 us
  waiting for transfers between devices  553 us (75%)
  matrix products  78.8 us (11%)
  starting transfers between devices  78.3 us (11%)
  local copies, waits for them, and re-layouts  14.4 us (2%)
  other arithmetic  7.56 us (1%)
    ppermute x127, waiting for transfers between devices, from_behind(): return lax.ppermute(value, axis, pairs)  535 us
    all_to_all x1, starting transfers between devices, per_device(): lax.all_to_all(value_out, 'tp', split_axis=0, concat_axis=1, tiled=True)  56.2 us
    dot_general x64, matrix products, attend(): jnp.einsum('kgrn,nkd->rkgd', score_grad, key_heads, preferred_element_typ...  19.5 us
    dot_general x64, matrix products, attend(): jnp.einsum('rkgd,nkd->kgrn', query_heads, key_heads, preferred_element_ty...  16.5 us
    dot_general x64, matrix products, attend(): jnp.einsum('rkgd,nkd->kgrn', grad_heads, value_heads, preferred_element_t...  14.9 us
  transfers between devices with their start and end apart: 131, of which 131 were waited for; matrix products, arithmetic and copies ran while one was open for 13% of the time, Pallas kernels for 0%

commit v1 on v0

v1 whole, which is shorter than its diff:
```python
import functools

import jax
import jax.numpy as jnp
from jax import lax
from jax.experimental import pallas as pl
from jax.experimental.pallas import tpu as pltpu
from jax.sharding import PartitionSpec as P

MESH = pl.DeviceIdType.MESH
HEAD_DIM = 128
GROUP = 8
TOK = 128
NX, NZ, NY, NT = 2, 8, 4, 4
ROWS = GROUP * TOK
SCALE = HEAD_DIM ** -0.5
LOG2E = 1.4426950408889634
NEG = -32768.0
BF = jnp.bfloat16
F32 = jnp.float32


def mm(a, b, dims):
    return lax.dot_general(a, b, (dims, ((), ())), preferred_element_type=F32)


def unit_order():
    order = [(0, 0), (-1, 0)] + ([(1, 0)] if NZ > 2 else [])
    order += [(0, 1), (-1, 1)] + ([(1, 1)] if NZ > 2 else [])
    for dist in range(2, NZ // 2 + 1):
        order += [(-dist, 0), (-dist, 1)]
        if dist < NZ // 2:
            order += [(dist, 0), (dist, 1)]
    return order


def pick(index, table):
    value = jnp.int32(table[0])
    for at, entry in enumerate(table):
        if at:
            value = jnp.where(index == at, jnp.int32(entry), value)
    return value


def split3(x):
    hi = x.astype(BF).astype(F32)
    mid = (x - hi).astype(BF).astype(F32)
    return hi, mid, x - hi - mid


def kernel(
    q_in, k_in, v_in, o_in, ln_in, do_in, bp,
    dq_out, dk_out, dv_out,
    kv, q2, dobuf, ld, qrow, dorow, qt, dot, dqt, acc, sendbuf, red1, s2buf, red2, fkv, rkv, dqs, rdq, kaug,
    kvy_s, kvy_r, do_s, do_r, q_s, q_r, ld_s, ld_r, f_s, f_r, b_s, b_r, s1_s, s1_r, s2_s, s2_r, kv_s, kv_r, dq_s, dq_r,
):
    ctx = lax.axis_index("ctx")
    t = lax.axis_index("tp")
    plane = NZ * NY
    xl = lax.div(ctx, plane)
    z = lax.rem(lax.div(ctx, NY), NZ)
    y = lax.rem(ctx, NY)
    xp = 1 - xl
    piece = TOK // NT

    def dev(x_, z_, y_, t_):
        return (x_ * plane + z_ * NY + y_, t_)

    def wrap(value, count):
        return lax.rem(value + count, count)

    group = [(dx, dt) for dx in range(NX) for dt in range(NT) if dx or dt]

    def group_dev(dx, dt):
        return dev(lax.rem(xl + dx, NX), z, y, lax.rem(t + dt, NT))

    barrier = pltpu.get_barrier_semaphore()
    peers = [group_dev(dx, dt) for dx, dt in group]
    peers += [dev(xl, z, lax.rem(y + dy, NY), t) for dy in range(1, NY)]
    peers += [dev(xl, lax.rem(z + dz, NZ), y, t) for dz in range(1, NZ)]
    for peer in peers:
        pl.semaphore_signal(barrier, inc=1, device_id=peer, device_id_type=MESH)
    pl.semaphore_wait(barrier, len(peers))

    def copy(src, dst, send, recv, device):
        return pltpu.make_async_remote_copy(
            src_ref=src, dst_ref=dst, send_sem=send, recv_sem=recv, device_id=device, device_id_type=MESH
        )

    def do_copy(dx, dt):
        tt = lax.rem(t + dt, NT)
        n = dx * NT + dt
        return copy(
            do_in.at[:, pl.ds(pl.multiple_of(tt * ROWS, ROWS), ROWS)],
            dobuf.at[dx, pl.ds(pl.multiple_of(t * piece, piece), piece), :],
            do_s.at[n], do_r.at[n], group_dev(dx, dt),
        )

    def kvy_copy(dy):
        return copy(kv.at[z, y], kv.at[z, y], kvy_s.at[dy], kvy_r.at[dy], dev(xl, z, lax.rem(y + dy, NY), t))

    def q_copy():
        return copy(q_in, q2, q_s.at[0], q_r.at[0], dev(xp, z, y, t))

    def ld_copy():
        return copy(ld.at[0], ld.at[1], ld_s.at[0], ld_r.at[0], dev(xp, z, y, t))

    def f_copy(step):
        row = wrap(z - step, NZ)
        return copy(kv.at[row], kv.at[row], f_s.at[step], f_r.at[step], dev(xl, lax.rem(z + 1, NZ), y, t))

    def b_copy(step):
        row = lax.rem(z + step, NZ)
        return copy(kv.at[row], kv.at[row], b_s.at[step], b_r.at[step], dev(xl, wrap(z - 1, NZ), y, t))

    def s1_copy(row, dy):
        yy = lax.rem(y + dy, NY)
        return copy(
            sendbuf.at[row, yy], red1.at[row, y], s1_s.at[row, dy], s1_r.at[row, dy], dev(xl, z, yy, t)
        )

    def s2_copy(row):
        return copy(s2buf.at[row], red2.at[z], s2_s.at[row], s2_r.at[z], dev(xl, row, y, t))

    def kvo_copy(dt):
        tt = lax.rem(t + dt, NT)
        rows = pl.ds(pl.multiple_of(tt * piece, piece), piece)
        return copy(fkv.at[:, rows, :], rkv.at[t], kv_s.at[dt], kv_r.at[dt], dev(xl, z, y, tt))

    def dq_copy(dx, dt):
        tt = lax.rem(t + dt, NT)
        n = dx * NT + dt
        rows = pl.ds(pl.multiple_of(tt * piece, piece), piece)
        return copy(dqs.at[dx, rows, :], rdq.at[dx, t], dq_s.at[n], dq_r.at[n], group_dev(dx, dt))

    for dt in range(1, NT):
        do_copy(0, dt).start()
    kv[z, y, 0] = k_in[...]
    kv[z, y, 1] = v_in[...]
    for dy in range(1, NY):
        kvy_copy(dy).start()
    for dt in range(NT):
        do_copy(1, dt).start()
    q_copy().start()
    dobuf[0, pl.ds(pl.multiple_of(t * piece, piece), piece), :] = do_in[
        :, pl.ds(pl.multiple_of(t * ROWS, ROWS), ROWS)
    ]

    sub16 = lax.broadcasted_iota(jnp.int32, (16, TOK), 0)
    tok16 = lax.broadcasted_iota(jnp.int32, (16, TOK), 1)

    def put_heads(half, src, rows_ref, cols_ref):
        for h in range(GROUP):
            blk = src[:, h * HEAD_DIM:(h + 1) * HEAD_DIM]
            at = slice(half * ROWS + h * TOK, half * ROWS + (h + 1) * TOK)
            rows_ref[at, :] = blk
            cols_ref[:HEAD_DIM, at] = blk.T

    def put_extra(half, base, cols_ref, hot):
        for h in range(GROUP):
            hi, mid, low = split3(ld[half, base + h:base + h + 1, :])
            tile = jnp.where(sub16 == 4 + 2 * half + tok16 // (TOK // 2), hot, 0.0)
            tile = jnp.where(sub16 == 0, hi, jnp.where(sub16 == 1, mid, jnp.where(sub16 == 2, low, tile)))
            at = slice(half * ROWS + h * TOK, half * ROWS + (h + 1) * TOK)
            cols_ref[HEAD_DIM:HEAD_DIM + 16, at] = tile.astype(BF)

    acc[...] = jnp.zeros_like(acc)
    dqt[...] = jnp.zeros_like(dqt)
    qt[HEAD_DIM:, :] = jnp.zeros_like(qt[HEAD_DIM:, :])
    dot[HEAD_DIM:, :] = jnp.zeros_like(dot[HEAD_DIM:, :])
    ld[0, :GROUP, :] = ln_in[...].T * (-1.0 / SCALE)
    put_heads(0, q_in, qrow, qt)
    put_extra(0, 0, qt, 1.0)

    lane = lax.broadcasted_iota(jnp.int32, (1, HEAD_DIM), 1)
    here, there = 2 * ctx, 2 * (xp * plane + z * NY + y)
    limit = jnp.full((1, HEAD_DIM), 1 << 20, jnp.int32)
    for at, half_block in enumerate((here, here + 1, there, there + 1)):
        limit = jnp.where(lane == 4 + at, bp[half_block], limit)

    def put_kaug(row, carry):
        for yy in range(NY):
            for hf in range(2):
                place = bp[2 * (xl * plane + row * NY + yy) + hf]
                line = jnp.where(lane < 3, 1.0, jnp.where(place > limit, NEG, 0.0))
                kaug[row, yy * TOK + hf * (TOK // 2):yy * TOK + (hf + 1) * (TOK // 2), :] = jnp.broadcast_to(
                    line, (TOK // 2, HEAD_DIM)
                ).astype(BF)
        return carry

    lax.fori_loop(0, NZ, put_kaug, 0)

    for dt in range(1, NT):
        do_copy(0, dt).wait_recv()
    put_heads(0, dobuf.at[0], dorow, dot)
    for h in range(GROUP):
        out_t = o_in[:, h * HEAD_DIM:(h + 1) * HEAD_DIM].T.astype(F32)
        grad_t = dot[:HEAD_DIM, h * TOK:(h + 1) * TOK].astype(F32)
        ld[0, GROUP + h:GROUP + h + 1, :] = -jnp.sum(out_t * grad_t, axis=0, keepdims=True)
    ld_copy().start()
    put_extra(0, GROUP, dot, 0.0)

    for dy in range(1, NY):
        kvy_copy(dy).wait_recv()
    f_copy(0).start()
    if NZ > 2:
        b_copy(0).start()

    n_keys = NY * TOK
    ones = jnp.where(lax.broadcasted_iota(jnp.int32, (n_keys, HEAD_DIM), 1) < 3, 1.0, 0.0).astype(BF)

    def unit(row, half, diagonal):
        cols = pl.ds(pl.multiple_of(half * ROWS, ROWS), ROWS)
        keys = kv[row, :, 0].reshape(n_keys, HEAD_DIM)
        values = kv[row, :, 1].reshape(n_keys, HEAD_DIM)
        s = mm(jnp.concatenate([keys, kaug[row]], axis=1), qt[:, cols], ((1,), (0,)))
        p = jnp.exp2(s * (SCALE * LOG2E))
        if diagonal:
            key_at = lax.broadcasted_iota(jnp.int32, (n_keys, ROWS), 0) - y * TOK
            query_at = lax.broadcasted_iota(jnp.int32, (n_keys, ROWS), 1) % TOK
            p = jnp.where((key_at > query_at) & (key_at <= (query_at | (TOK // 2 - 1))), 0.0, p)
        dp = mm(jnp.concatenate([values, ones], axis=1), dot[:, cols], ((1,), (0,)))
        ds = (p * dp).astype(BF)
        acc[row, 1] += mm(p.astype(BF), dorow[cols, :], ((1,), (0,)))
        acc[row, 0] += mm(ds, qrow[cols, :], ((1,), (0,)))
        dqt[:, cols] += mm(keys, ds, ((0,), (0,)))

    def send_row(row):
        for yy in range(NY):
            sendbuf[row, yy] = acc[row, :, yy * TOK:(yy + 1) * TOK, :].astype(BF)
        for dy in range(1, NY):
            s1_copy(row, dy).start()

    def sum_row(row, own):
        for dy in range(1, NY):
            s1_copy(row, dy).wait_recv()
        total = acc[row, :, pl.ds(pl.multiple_of(y * TOK, TOK), TOK), :]
        for dy in range(1, NY):
            total = total + red1[row, lax.rem(y + dy, NY)].astype(F32)
        if own:
            acc[row, :, pl.ds(pl.multiple_of(y * TOK, TOK), TOK), :] = total
        else:
            s2buf[row] = total.astype(BF)
            s2_copy(row).start()

    order = unit_order()
    rels, halves = [r for r, _ in order], [h for _, h in order]
    seen, done_at = set(), {}
    for at, (rel, _) in enumerate(order):
        if rel in seen:
            done_at[rel] = at
        seen.add(rel)
    finished = sorted(done_at, key=done_at.get)
    first_partner = halves.index(1)

    unit(z, 0, True)

    def step(u, carry):
        row = wrap(z + pick(u, rels), NZ)
        half = pick(u, halves)

        for dist in range(1, NZ // 2 + 1):
            @pl.when(u == rels.index(-dist))
            def _():
                f_copy(dist - 1).wait_recv()
                if dist < NZ // 2:
                    f_copy(dist).start()
                    b_copy(dist - 1).wait_recv()
                    if dist < NZ // 2 - 1:
                        b_copy(dist).start()

        @pl.when(u == first_partner)
        def _():
            for dt in range(NT):
                do_copy(1, dt).wait_recv()
            q_copy().wait_recv()
            ld_copy().wait_recv()
            put_heads(1, q2, qrow, qt)
            put_extra(1, 0, qt, 1.0)
            put_heads(1, dobuf.at[1], dorow, dot)
            put_extra(1, GROUP, dot, 0.0)

        unit(row, half, False)

        @pl.when(half == 1)
        def _():
            send_row(row)

        for at, rel in enumerate(finished[:-1]):
            @pl.when(u == done_at[finished[at + 1]])
            def _():
                sum_row(wrap(z + rel, NZ), rel == 0)

        return carry

    lax.fori_loop(1, len(order), step, 0)

    for half in (1, 0):
        for h in range(GROUP):
            at = slice(half * ROWS + h * TOK, half * ROWS + (h + 1) * TOK)
            dqs[half, :, h * HEAD_DIM:(h + 1) * HEAD_DIM] = (dqt[:, at].T * SCALE).astype(BF)
        for dt in range(NT):
            if half or dt:
                dq_copy(half, dt).start()
    rdq[0, t] = dqs[0, pl.ds(pl.multiple_of(t * piece, piece), piece), :]

    sum_row(wrap(z + finished[-1], NZ), False)
    total = acc[z, :, pl.ds(pl.multiple_of(y * TOK, TOK), TOK), :]
    for dz in range(1, NZ):
        s2_copy_back = copy(
            s2buf.at[z], red2.at[lax.rem(z + dz, NZ)], s2_s.at[z], s2_r.at[lax.rem(z + dz, NZ)], dev(xl, z, y, t)
        )
        s2_copy_back.wait_recv()
        total = total + red2[lax.rem(z + dz, NZ)].astype(F32)
    fkv[0] = (total[0] * SCALE).astype(BF)
    fkv[1] = total[1].astype(BF)
    for dt in range(1, NT):
        kvo_copy(dt).start()
    rkv[t] = fkv[:, pl.ds(pl.multiple_of(t * piece, piece), piece), :]

    for dx, dt in group:
        dq_copy(dx, dt).wait_recv()
    for tt in range(NT):
        dq_out[:, tt * ROWS:(tt + 1) * ROWS] = (rdq[0, tt].astype(F32) + rdq[1, tt].astype(F32)).astype(BF)
    for dt in range(1, NT):
        kvo_copy(dt).wait_recv()
    for tt in range(NT):
        dk_out[:, tt * HEAD_DIM:(tt + 1) * HEAD_DIM] = rkv[tt, 0]
        dv_out[:, tt * HEAD_DIM:(tt + 1) * HEAD_DIM] = rkv[tt, 1]

    for dx, dt in group:
        do_copy(dx, dt).wait_send()
        dq_copy(dx, dt).wait_send()
    for dy in range(1, NY):
        kvy_copy(dy).wait_send()
    q_copy().wait_send()
    ld_copy().wait_send()
    for s in range(NZ // 2):
        f_copy(s).wait_send()
    for s in range(NZ // 2 - 1):
        b_copy(s).wait_send()
    for dz in range(NZ):
        row = lax.rem(z + dz, NZ)
        for dy in range(1, NY):
            s1_copy(row, dy).wait_send()
        if dz:
            s2_copy(row).wait_send()
    for dt in range(1, NT):
        kvo_copy(dt).wait_send()


def per_device(queries, key_rows, value_rows, attn_out, log_norm, grad_out, block_pos):
    piece = TOK // NT
    vmem = pl.BlockSpec(memory_space=pltpu.VMEM)
    dma = pltpu.SemaphoreType.DMA
    blk = (2, TOK, HEAD_DIM)
    return pl.pallas_call(
        kernel,
        out_shape=[
            jax.ShapeDtypeStruct((piece, NT * ROWS), BF),
            jax.ShapeDtypeStruct((piece, NT * HEAD_DIM), BF),
            jax.ShapeDtypeStruct((piece, NT * HEAD_DIM), BF),
        ],
        in_specs=[vmem] * 6 + [pl.BlockSpec(memory_space=pltpu.SMEM)],
        out_specs=[vmem] * 3,
        scratch_shapes=[
            pltpu.VMEM((NZ, NY) + blk, BF),
            pltpu.VMEM((TOK, ROWS), BF),
            pltpu.VMEM((2, TOK, ROWS), BF),
            pltpu.VMEM((2, 2 * GROUP, TOK), F32),
            pltpu.VMEM((2 * ROWS, HEAD_DIM), BF),
            pltpu.VMEM((2 * ROWS, HEAD_DIM), BF),
            pltpu.VMEM((2 * HEAD_DIM, 2 * ROWS), BF),
            pltpu.VMEM((2 * HEAD_DIM, 2 * ROWS), BF),
            pltpu.VMEM((HEAD_DIM, 2 * ROWS), F32),
            pltpu.VMEM((NZ, 2, NY * TOK, HEAD_DIM), F32),
            pltpu.VMEM((NZ, NY) + blk, BF),
            pltpu.VMEM((NZ, NY) + blk, BF),
            pltpu.VMEM((NZ,) + blk, BF),
            pltpu.VMEM((NZ,) + blk, BF),
            pltpu.VMEM(blk, BF),
            pltpu.VMEM((NT, 2, piece, HEAD_DIM), BF),
            pltpu.VMEM((2, TOK, ROWS), BF),
            pltpu.VMEM((2, NT, piece, ROWS), BF),
            pltpu.VMEM((NZ, NY * TOK, HEAD_DIM), BF),
            dma((NY,)), dma((NY,)), dma((2 * NT,)), dma((2 * NT,)), dma((1,)), dma((1,)), dma((1,)), dma((1,)),
            dma((NZ // 2,)), dma((NZ // 2,)), dma((NZ // 2,)), dma((NZ // 2,)), dma((NZ, NY)), dma((NZ, NY)),
            dma((NZ,)), dma((NZ,)), dma((NT,)), dma((NT,)), dma((2 * NT,)), dma((2 * NT,)),
        ],
        compiler_params=pltpu.CompilerParams(
            collective_id=0, has_side_effects=True, vmem_limit_bytes=52 * 2**20
        ),
    )(queries, key_rows, value_rows, attn_out, log_norm, grad_out, block_pos)


def solution(mesh):
    split = P("ctx", "tp")
    joint = P(("ctx", "tp"), None)
    return jax.shard_map(
        per_device,
        mesh=mesh,
        in_specs=(split, split, split, split, split, joint, P()),
        out_specs=(joint, joint, joint),
        check_vma=False,
    )
```

time: 740 us -> 77.8 us (0.11)
  waiting for transfers between devices: 553 us -> 0 us
  matrix products: 78.8 us -> 0 us
  starting transfers between devices: 78.3 us -> 0 us
  Pallas kernels: 0 us -> 71.3 us
  local copies, waits for them, and re-layouts: 14.4 us -> 5.6 us
  other arithmetic: 7.56 us -> 0 us
    ppermute x127 -> x0, waiting for transfers between devices: 535 us -> none  [from_behind(): return lax.ppermute(value, axis, pairs)]
    dot_general x320 -> x0, matrix products: 78.8 us -> none  [the longest x64 19.5 us: attend(): jnp.einsum('kgrn,nkd->rkgd', score_grad, key_heads, preferred_element_typ...]
    pallas_call x0 -> x1, Pallas kernels: none -> 71.3 us  [per_device(): pl.pallas_call(kernel, out_shape=[jax.ShapeDtypeStruct((piece, NT * ROWS)...]
    all_to_all x4 -> x0, starting transfers between devices: 71.1 us -> none  [the longest x1 56.2 us: per_device(): lax.all_to_all(value_out, 'tp', split_axis=0, concat_axis=1, tiled=True)]
    all_to_all x4 -> x0, waiting for transfers between devices: 17.8 us -> none  [the longest x1 6.06 us: per_device(): lax.all_to_all(query_out, 'tp', split_axis=0, concat_axis=1, tiled=True)]
  transfers between devices with their start and end apart: 131 -> 0, of which waited for: 131 -> 0; matrix products, arithmetic and copies ran while one was open for 13% -> 0% of each run, Pallas kernels for 0% -> 0%
where the time goes in v1:
time: 77.8 us; the launch traced here: 77.6 us
  Pallas kernels  71.3 us (92%)
  local copies, waits for them, and re-layouts  5.6 us (7%)
    pallas_call x1, Pallas kernels, per_device(): pl.pallas_call(kernel, out_shape=[jax.ShapeDtypeStruct((piece, NT * ROWS)...  71.3 us
    unnamed x16, local copies, waits for them, and re-layouts  5.6 us

profile of v1, /device:TPU:1, one launch (start us, length us, event | category | flops | bytes accessed | tf_op | source)
XLA Modules:
  0.0 77.6 jit_solution(229049260947073549)
XLA Ops:
  0.6 0.0 copy-start.5
  0.6 0.0 copy-start.4
  0.7 0.0 copy-start.3
  0.7 0.8 %copy.10.ln_in = f32[128,8]{1,0:T(8,128)S(1)} copy(f32[128,8]{0,1:T(8,128)} %param.11) | data formatting | bytes 8192 | tf_op args[4]
  1.5 0.0 copy-done.5
  1.5 0.0 copy-done.4
  1.5 0.0 copy-done.3
  1.5 0.0 copy-start
  1.5 0.9 %copy-done = bf16[128,1024]{1,0:T(8,128)(2,1)S(1)} copy-done((bf16[128,1024]{1,0:T(8,128)(2,1)S(1)}, bf16[128,1024]{1,0:T(8,128)(2,1)}, u32[]{:S(2)}) %copy-start) | copy-done | bytes 262168
  2.4 0.0 copy-start.1
  2.4 0.9 %copy-done.1 = bf16[128,1024]{1,0:T(8,128)(2,1)S(1)} copy-done((bf16[128,1024]{1,0:T(8,128)(2,1)S(1)}, bf16[128,1024]{1,0:T(8,128)(2,1)}, u32[]{:S(2)}) %copy-start.1) | copy-done | bytes 262168
  3.4 0.0 copy-start.2
  3.4 0.9 %copy-done.2 = bf16[32,4096]{1,0:T(8,128)(2,1)S(1)} copy-done((bf16[32,4096]{1,0:T(8,128)(2,1)S(1)}, bf16[32,4096]{1,0:T(8,128)(2,1)}, u32[]{:S(2)}) %copy-start.2) | copy-done | bytes 262168
  4.3 71.3 %shard_map.94 = (bf16[32,4096]{1,0:T(8,128)(2,1)S(1)}, bf16[32,512]{1,0:T(8,128)(2,1)S(1)}, bf16[32,512]{1,0:T(8,128)(2,1)S(1)}) custom-call(bf16[128,1024]{1,0:T(8,128)(2,1)S(1)} %copy-done, bf16[128,128]{1,0:T(8,128)(2,1)S(1)} %copy-done.3, bf16[128,128]{1,0:T(8,128)(2,1)S(1)} %copy-done.4, bf16[128,1024]{1,0:T(8,128)(2,1)S(1)} %copy-done.1, ...), custom_call_target="tpu_custom_call" | custom-call | tf_op jit(solution)/shard_map/pallas_call | solution.py:357
  75.7 0.7 copy.14
  76.4 0.6 copy.15
  77.0 0.6 copy.16
Async XLA Ops:
  0.6 0.8 %copy-start.5 = (s32[128]{0:T(128)S(1)}, s32[128]{0:T(128)}, u32[]{:S(2)}) copy-start(s32[128]{0:T(128)} %bp.1) | copy-start | bytes 1540
  0.6 0.8 %copy-start.4 = (bf16[128,128]{1,0:T(8,128)(2,1)S(1)}, bf16[128,128]{1,0:T(8,128)(2,1)}, u32[]{:S(2)}) copy-start(bf16[128,128]{1,0:T(8,128)(2,1)} %v_in.1) | copy-start | bytes 98308
  0.7 0.8 %copy-start.3 = (bf16[128,128]{1,0:T(8,128)(2,1)S(1)}, bf16[128,128]{1,0:T(8,128)(2,1)}, u32[]{:S(2)}) copy-start(bf16[128,128]{1,0:T(8,128)(2,1)} %k_in.1) | copy-start | bytes 98308
  1.5 1.0 %copy-start = (bf16[128,1024]{1,0:T(8,128)(2,1)S(1)}, bf16[128,1024]{1,0:T(8,128)(2,1)}, u32[]{:S(2)}) copy-start(bf16[128,1024]{1,0:T(8,128)(2,1)} %q_in.1) | copy-start | bytes 786436
  2.4 0.9 %copy-start.1 = (bf16[128,1024]{1,0:T(8,128)(2,1)S(1)}, bf16[128,1024]{1,0:T(8,128)(2,1)}, u32[]{:S(2)}) copy-start(bf16[128,1024]{1,0:T(8,128)(2,1)} %o_in.1) | copy-start | bytes 786436
  3.4 0.9 %copy-start.2 = (bf16[32,4096]{1,0:T(8,128)(2,1)S(1)}, bf16[32,4096]{1,0:T(8,128)(2,1)}, u32[]{:S(2)}) copy-start(bf16[32,4096]{1,0:T(8,128)(2,1)} %do_in.1) | copy-start | bytes 786436

commit v2 on v1

v2 whole, which is shorter than its diff:
```python
import functools

import jax
import jax.numpy as jnp
from jax import lax
from jax.experimental import pallas as pl
from jax.experimental.pallas import tpu as pltpu
from jax.sharding import PartitionSpec as P

MESH = pl.DeviceIdType.MESH
HEAD_DIM = 128
GROUP = 8
TOK = 128
NX, NZ, NY, NT = 2, 8, 4, 4
LAG = 3
ROWS = GROUP * TOK
SCALE = HEAD_DIM ** -0.5
LOG2E = 1.4426950408889634
NEG = -32768.0
BF = jnp.bfloat16
F32 = jnp.float32


def mm(a, b, dims):
    return lax.dot_general(a, b, (dims, ((), ())), preferred_element_type=F32)


def unit_order():
    if NZ != 8:
        rels = [0] + [rel for d in range(1, NZ // 2 + 1) for rel in ((-d, d) if d < NZ // 2 else (-d,))]
        return [(rel, half) for half in range(2) for rel in (rels, rels[::-1])[half]]
    near = [(0, 0), (-1, 0), (1, 0), (-1, 1), (-2, 0), (2, 0), (-2, 1), (2, 1)]
    return near + [(-3, 0), (3, 0), (-3, 1), (3, 1), (-4, 0), (-4, 1), (1, 1), (0, 1)]


def pick(index, table):
    value = jnp.int32(table[0])
    for at, entry in enumerate(table):
        if at:
            value = jnp.where(index == at, jnp.int32(entry), value)
    return value


def split3(x):
    hi = x.astype(BF).astype(F32)
    mid = (x - hi).astype(BF).astype(F32)
    return hi, mid, x - hi - mid


def kernel(
    q_hbm, k_in, v_in, o_hbm, ln_in, do_in, bp_in,
    dq_out, dk_out, dv_out,
    q_in, o_in, bp, kk, vv, q2, dobuf, ld, qrow, dorow, qt, dot, dqt, acc, sendbuf, red1, s2buf, fin, dqs, rdq, kaug,
    loc, ky_s, ky_r, vz_s, vz_r, vy_s, vy_r, do_s, do_r, q_s, q_r, ld_s, ld_r, ring_s, ring_r, s1_s, s1_r, s2_s, s2_r, kv_s, kv_r, dq_s, dq_r,
):
    ctx = lax.axis_index("ctx")
    t = lax.axis_index("tp")
    plane = NZ * NY
    xl = lax.div(ctx, plane)
    z = lax.rem(lax.div(ctx, NY), NZ)
    y = lax.rem(ctx, NY)
    xp = 1 - xl
    piece = TOK // NT

    def dev(x_, z_, y_, t_):
        return (x_ * plane + z_ * NY + y_, t_)

    def wrap(value, count):
        return lax.rem(value + count, count)

    group = [(dx, dt) for dx in range(NX) for dt in range(NT) if dx or dt]

    def group_dev(dx, dt):
        return dev(lax.rem(xl + dx, NX), z, y, lax.rem(t + dt, NT))

    barrier = pltpu.get_barrier_semaphore()
    peers = [group_dev(dx, dt) for dx, dt in group]
    peers += [dev(xl, z, lax.rem(y + dy, NY), t) for dy in range(1, NY)]
    peers += [dev(xl, lax.rem(z + dz, NZ), y, t) for dz in range(1, NZ)]
    for peer in peers:
        pl.semaphore_signal(barrier, inc=1, device_id=peer, device_id_type=MESH)

    fetches = [
        pltpu.make_async_copy(src, dst, loc.at[at])
        for at, (src, dst) in enumerate([
            (k_in, kk.at[z, 0]),
            (v_in, vv.at[z, 0]),
            (q_hbm, q_in),
            (ln_in, ld.at[0, :GROUP, :]),
            (bp_in, bp),
            (o_hbm, o_in),
            (
                do_in.at[:, pl.ds(pl.multiple_of(t * ROWS, ROWS), ROWS)],
                dobuf.at[0, pl.ds(pl.multiple_of(t * piece, piece), piece), :],
            ),
        ])
    ]
    for fetch in fetches:
        fetch.start()
    pl.semaphore_wait(barrier, len(peers))

    def copy(src, dst, send, recv, device):
        return pltpu.make_async_remote_copy(
            src_ref=src, dst_ref=dst, send_sem=send, recv_sem=recv, device_id=device, device_id_type=MESH
        )

    def settle(ref, sem):
        pltpu.make_async_copy(ref, ref, sem).wait()

    def do_copy(dx, dt):
        tt = lax.rem(t + dt, NT)
        return copy(
            do_in.at[:, pl.ds(pl.multiple_of(tt * ROWS, ROWS), ROWS)],
            dobuf.at[dx, pl.ds(pl.multiple_of(t * piece, piece), piece), :],
            do_s.at[dx], do_r.at[dx], group_dev(dx, dt),
        )

    def ky_copy(dy):
        return copy(kk.at[z, 0], kk.at[z, dy], ky_s.at[0], ky_r.at[0], dev(xl, z, lax.rem(y + dy, NY), t))

    def vz_copy(dz):
        dist = min(dz, NZ - dz)
        return copy(vv.at[z, 0], vv.at[z, 0], vz_s.at[0], vz_r.at[dist], dev(xl, lax.rem(z + dz, NZ), y, t))

    def vy_copy(row, dy):
        return copy(vv.at[row, 0], vv.at[row, dy], vy_s.at[0], vy_r.at[row], dev(xl, z, lax.rem(y + dy, NY), t))

    def q_copy():
        return copy(q_hbm, q2, q_s.at[0], q_r.at[0], dev(xp, z, y, t))

    def ld_copy():
        return copy(ld.at[0], ld.at[1], ld_s.at[0], ld_r.at[0], dev(xp, z, y, t))

    def ring_copy(step, back):
        row = lax.rem(z + step, NZ) if back else wrap(z - step, NZ)
        to = wrap(z - 1, NZ) if back else lax.rem(z + 1, NZ)
        part = pl.ds(0, NY) if step < NZ // 2 - 1 else pl.ds(back * NY // 2, NY // 2)
        return copy(kk.at[row, part], kk.at[row, part], ring_s.at[0], ring_r.at[step], dev(xl, to, y, t))

    def s1_copy(row, dy):
        return copy(
            sendbuf.at[row, dy - 1], red1.at[row, dy - 1], s1_s.at[0], s1_r.at[row], dev(xl, z, wrap(y - dy, NY), t)
        )

    def s2_copy(row, dt):
        tt = lax.rem(t + dt, NT)
        rows = pl.ds(pl.multiple_of(tt * piece, piece), piece)
        from_there = wrap(z - row, NZ) - 1
        return copy(s2buf.at[row, :, rows, :], fin.at[from_there, t], s2_s.at[0], s2_r.at[0], dev(xl, row, y, tt))

    def own_copy(dy, dt):
        tt = lax.rem(t + dt, NT)
        rows = pl.ds(pl.multiple_of(tt * piece, piece), piece)
        src = sendbuf.at[z, dy - 1, :, rows, :] if dy else s2buf.at[z, :, rows, :]
        n = min(dy, 1)
        return copy(src, fin.at[NZ - 1 + dy, t], kv_s.at[n], kv_r.at[n], dev(xl, z, wrap(y - dy, NY), tt))

    def dq_copy(dx, dt):
        tt = lax.rem(t + dt, NT)
        rows = pl.ds(pl.multiple_of(tt * piece, piece), piece)
        return copy(dqs.at[dx, rows, :], rdq.at[dx, t], dq_s.at[dx], dq_r.at[dx], group_dev(dx, dt))

    for dt in range(1, NT):
        do_copy(0, dt).start()
    fetches[0].wait()
    fetches[1].wait()

    for dy in range(1, NY):
        ky_copy(dy).start()
    near_first = [dz for _, dz in sorted((min(dz, NZ - dz), dz) for dz in range(1, NZ))]
    for dy in range(1, NY):
        vy_copy(z, dy).start()
    for dz in near_first[:2]:
        vz_copy(dz).start()

    sub16 = lax.broadcasted_iota(jnp.int32, (16, TOK), 0)
    tok16 = lax.broadcasted_iota(jnp.int32, (16, TOK), 1)

    def put_heads(half, src, rows_ref, cols_ref):
        for h in range(GROUP):
            blk = src[:, h * HEAD_DIM:(h + 1) * HEAD_DIM]
            at = slice(half * ROWS + h * TOK, half * ROWS + (h + 1) * TOK)
            rows_ref[at, :] = blk
            cols_ref[:HEAD_DIM, at] = blk.T

    def put_extra(half, base, cols_ref, hot):
        for h in range(GROUP):
            hi, mid, low = split3(ld[half, base + h:base + h + 1, :])
            tile = jnp.where(sub16 == 4 + 2 * half + tok16 // (TOK // 2), hot, 0.0)
            tile = jnp.where(sub16 == 0, hi, jnp.where(sub16 == 1, mid, jnp.where(sub16 == 2, low, tile)))
            at = slice(half * ROWS + h * TOK, half * ROWS + (h + 1) * TOK)
            cols_ref[HEAD_DIM:HEAD_DIM + 16, at] = tile.astype(BF)

    acc[...] = jnp.zeros_like(acc)
    dqt[...] = jnp.zeros_like(dqt)
    qt[HEAD_DIM:, :] = jnp.zeros_like(qt[HEAD_DIM:, :])
    dot[HEAD_DIM:, :] = jnp.zeros_like(dot[HEAD_DIM:, :])
    for fetch in fetches[2:5]:
        fetch.wait()
    ld[0, :GROUP, :] = ld[0, :GROUP, :] * (-1.0 / SCALE)
    put_heads(0, q_in, qrow, qt)
    put_extra(0, 0, qt, 1.0)

    lane = lax.broadcasted_iota(jnp.int32, (1, HEAD_DIM), 1)
    here, there = 2 * ctx, 2 * (xp * plane + z * NY + y)
    limit = jnp.full((1, HEAD_DIM), 1 << 20, jnp.int32)
    for at, half_block in enumerate((here, here + 1, there, there + 1)):
        limit = jnp.where(lane == 4 + at, bp[half_block], limit)

    def put_kaug(row, carry):
        for yy in range(NY):
            for hf in range(2):
                place = bp[2 * (xl * plane + row * NY + wrap(y - yy, NY)) + hf]
                line = jnp.where(lane < 3, 1.0, jnp.where(place > limit, NEG, 0.0))
                kaug[row, yy * TOK + hf * (TOK // 2):yy * TOK + (hf + 1) * (TOK // 2), :] = jnp.broadcast_to(
                    line, (TOK // 2, HEAD_DIM)
                ).astype(BF)
        return carry

    lax.fori_loop(0, NZ, put_kaug, 0)
    for dt in range(NT):
        do_copy(1, dt).start()
    q_copy().start()
    for dz in near_first[2:]:
        vz_copy(dz).start()

    settle(kk.at[z, 1:], ky_r.at[0])
    ring_copy(0, 0).start()
    ring_copy(0, 1).start()

    def pass_values(dist):
        both = sorted({dist, NZ - dist})
        settle(vv.at[:len(both), 0], vz_r.at[dist])
        for dz in both:
            for dy in range(1, NY):
                vy_copy(wrap(z - dz, NZ), dy).start()

    def pass_keys(dist):
        settle(kk.at[:2 if dist < NZ // 2 else 1], ring_r.at[dist - 1])
        if dist < NZ // 2:
            ring_copy(dist, 0).start()
            ring_copy(dist, 1).start()

    pass_values(1)
    pass_keys(1)
    for fetch in fetches[5:]:
        fetch.wait()
    if NT > 1:
        settle(dobuf.at[0, :(NT - 1) * piece], do_r.at[0])
    put_heads(0, dobuf.at[0], dorow, dot)
    for h in range(GROUP):
        out_t = o_in[:, h * HEAD_DIM:(h + 1) * HEAD_DIM].T.astype(F32)
        grad_t = dot[:HEAD_DIM, h * TOK:(h + 1) * TOK].astype(F32)
        ld[0, GROUP + h:GROUP + h + 1, :] = -jnp.sum(out_t * grad_t, axis=0, keepdims=True)
    ld_copy().start()
    put_extra(0, GROUP, dot, 0.0)

    n_keys = NY * TOK
    ones = jnp.where(lax.broadcasted_iota(jnp.int32, (n_keys, HEAD_DIM), 1) < 3, 1.0, 0.0).astype(BF)

    def unit(row, half, diagonal):
        cols = pl.ds(pl.multiple_of(half * ROWS, ROWS), ROWS)
        keys = kk[row].reshape(n_keys, HEAD_DIM)
        values = vv[row].reshape(n_keys, HEAD_DIM)
        s = mm(jnp.concatenate([keys, kaug[row]], axis=1), qt[:, cols], ((1,), (0,)))
        p = jnp.exp2(s * (SCALE * LOG2E))
        if diagonal:
            key_at = lax.broadcasted_iota(jnp.int32, (TOK, ROWS), 0)
            query_at = lax.broadcasted_iota(jnp.int32, (TOK, ROWS), 1) % TOK
            later = (key_at > query_at) & (key_at <= (query_at | (TOK // 2 - 1)))
            p = jnp.concatenate([jnp.where(later, 0.0, p[:TOK]), p[TOK:]], axis=0)
        dp = mm(jnp.concatenate([values, ones], axis=1), dot[:, cols], ((1,), (0,)))
        ds = (p * dp).astype(BF)
        acc[row, 1] += mm(p.astype(BF), dorow[cols, :], ((1,), (0,)))
        acc[row, 0] += mm(ds, qrow[cols, :], ((1,), (0,)))
        dqt[:, cols] += mm(keys, ds, ((0,), (0,)))

    def send_row(row, own):
        for dy in range(1, NY):
            sendbuf[row, dy - 1] = acc[row, :, dy * TOK:(dy + 1) * TOK, :].astype(BF)
            if own:
                for dt in range(NT):
                    own_copy(dy, dt).start()
            else:
                s1_copy(row, dy).start()
        if own:
            s2buf[row] = acc[row, :, :TOK, :].astype(BF)
            for dt in range(1, NT):
                own_copy(0, dt).start()

    def sum_row(row):
        settle(red1.at[row], s1_r.at[row])
        total = acc[row, :, :TOK, :]
        for dy in range(1, NY):
            total = total + red1[row, dy - 1].astype(F32)
        s2buf[row] = total.astype(BF)
        for dt in range(NT):
            s2_copy(row, dt).start()

    order = unit_order()
    rels, halves = [r for r, _ in order], [h for _, h in order]
    seen, done_at = set(), {}
    for at, (rel, _) in enumerate(order):
        if rel in seen:
            done_at[rel] = at
        seen.add(rel)
    finished = sorted(done_at, key=done_at.get)
    first_partner = halves.index(1)
    summed_inside = [rel for rel in finished if rel and done_at[rel] + LAG < len(order)]

    settle(vv.at[z, 1:], vy_r.at[z])
    unit(z, 0, True)

    def send_query_grad(half):
        for h in range(GROUP):
            at = slice(half * ROWS + h * TOK, half * ROWS + (h + 1) * TOK)
            dqs[half, :, h * HEAD_DIM:(h + 1) * HEAD_DIM] = (dqt[:, at].T * SCALE).astype(BF)
        for dt in range(NT):
            if half or dt:
                dq_copy(half, dt).start()
        if not half:
            rdq[0, t] = dqs[0, pl.ds(pl.multiple_of(t * piece, piece), piece), :]

    def step(u, carry):
        row = wrap(z + pick(u, rels), NZ)
        half = pick(u, halves)

        for dist in range(1, NZ // 2 + 1):
            @pl.when(u == rels.index(-dist))
            def _():
                if dist > 1:
                    pass_keys(dist)
                if dist + 1 <= NZ // 2:
                    pass_values(dist + 1)
                for dz in sorted({dist, NZ - dist}):
                    row = wrap(z - dz, NZ)
                    settle(vv.at[row, 1:], vy_r.at[row])

        @pl.when(u == first_partner)
        def _():
            settle(dobuf.at[1], do_r.at[1])
            q_copy().wait_recv()
            ld_copy().wait_recv()
            put_heads(1, q2, qrow, qt)
            put_extra(1, 0, qt, 1.0)
            put_heads(1, dobuf.at[1], dorow, dot)
            put_extra(1, GROUP, dot, 0.0)

        unit(row, half, False)

        @pl.when(u == len(order) - 1 - halves[::-1].index(0))
        def _():
            send_query_grad(0)

        for rel in finished:
            @pl.when(u == done_at[rel])
            def _():
                send_row(wrap(z + rel, NZ), rel == 0)

            if rel in summed_inside:
                @pl.when(u == done_at[rel] + LAG)
                def _():
                    sum_row(wrap(z + rel, NZ))

        return carry

    lax.fori_loop(1, len(order), step, 0)

    send_query_grad(1)
    for rel in finished:
        if rel and rel not in summed_inside:
            sum_row(wrap(z + rel, NZ))
    fin[NZ - 1, t] = s2buf[z, :, pl.ds(pl.multiple_of(t * piece, piece), piece), :]

    if NT > 1:
        settle(rdq.at[0, :NT - 1], dq_r.at[0])
    settle(rdq.at[1], dq_r.at[1])
    for tt in range(NT):
        dq_out[:, tt * ROWS:(tt + 1) * ROWS] = (rdq[0, tt].astype(F32) + rdq[1, tt].astype(F32)).astype(BF)
    if NT > 1:
        settle(fin.at[0, :NT - 1], kv_r.at[0])
    settle(fin.at[NZ:], kv_r.at[1])
    settle(fin.at[:NZ - 1], s2_r.at[0])
    for tt in range(NT):
        total = fin[0, tt].astype(F32)
        for n in range(1, NZ + NY - 1):
            total = total + fin[n, tt].astype(F32)
        dk_out[:, tt * HEAD_DIM:(tt + 1) * HEAD_DIM] = (total[0] * SCALE).astype(BF)
        dv_out[:, tt * HEAD_DIM:(tt + 1) * HEAD_DIM] = total[1].astype(BF)

    if NT > 1:
        settle(dobuf.at[0, :(NT - 1) * piece], do_s.at[0])
        settle(rdq.at[0, :NT - 1], dq_s.at[0])
        settle(fin.at[0, :NT - 1], kv_s.at[0])
    settle(dobuf.at[1], do_s.at[1])
    settle(rdq.at[1], dq_s.at[1])
    settle(kk.at[0, 1:], ky_s.at[0])
    settle(vv.at[1:, 0], vz_s.at[0])
    settle(vv.at[:, 1:], vy_s.at[0])
    settle(kk.at[1:], ring_s.at[0])
    settle(red1.at[1:], s1_s.at[0])
    settle(fin.at[NZ:], kv_s.at[1])
    settle(fin.at[:NZ - 1], s2_s.at[0])
    q_copy().wait_send()
    ld_copy().wait_send()


def per_device(queries, key_rows, value_rows, attn_out, log_norm, grad_out, block_pos):
    piece = TOK // NT
    vmem = pl.BlockSpec(memory_space=pltpu.VMEM)
    dma = pltpu.SemaphoreType.DMA
    blk = (2, TOK, HEAD_DIM)
    return pl.pallas_call(
        kernel,
        out_shape=[
            jax.ShapeDtypeStruct((piece, NT * ROWS), BF),
            jax.ShapeDtypeStruct((piece, NT * HEAD_DIM), BF),
            jax.ShapeDtypeStruct((piece, NT * HEAD_DIM), BF),
        ],
        in_specs=[pl.BlockSpec(memory_space=pltpu.HBM)] * 7,
        out_specs=[vmem] * 3,
        scratch_shapes=[
            pltpu.VMEM((TOK, ROWS), BF),
            pltpu.VMEM((TOK, ROWS), BF),
            pltpu.SMEM((2 * NX * NZ * NY,), jnp.int32),
            pltpu.VMEM((NZ, NY, TOK, HEAD_DIM), BF),
            pltpu.VMEM((NZ, NY, TOK, HEAD_DIM), BF),
            pltpu.VMEM((TOK, ROWS), BF),
            pltpu.VMEM((2, TOK, ROWS), BF),
            pltpu.VMEM((2, 2 * GROUP, TOK), F32),
            pltpu.VMEM((2 * ROWS, HEAD_DIM), BF),
            pltpu.VMEM((2 * ROWS, HEAD_DIM), BF),
            pltpu.VMEM((2 * HEAD_DIM, 2 * ROWS), BF),
            pltpu.VMEM((2 * HEAD_DIM, 2 * ROWS), BF),
            pltpu.VMEM((HEAD_DIM, 2 * ROWS), F32),
            pltpu.VMEM((NZ, 2, NY * TOK, HEAD_DIM), F32),
            pltpu.VMEM((NZ, NY - 1) + blk, BF),
            pltpu.VMEM((NZ, NY - 1) + blk, BF),
            pltpu.VMEM((NZ,) + blk, BF),
            pltpu.VMEM((NZ + NY - 1, NT, 2, piece, HEAD_DIM), BF),
            pltpu.VMEM((2, TOK, ROWS), BF),
            pltpu.VMEM((2, NT, piece, ROWS), BF),
            pltpu.VMEM((NZ, NY * TOK, HEAD_DIM), BF),
            dma((7,)), dma((1,)), dma((1,)), dma((1,)), dma((NZ,)), dma((1,)), dma((NZ,)), dma((2,)), dma((2,)),
            dma((1,)), dma((1,)), dma((1,)), dma((1,)), dma((1,)), dma((NZ,)), dma((1,)), dma((NZ,)),
            dma((1,)), dma((1,)), dma((2,)), dma((2,)), dma((2,)), dma((2,)),
        ],
        compiler_params=pltpu.CompilerParams(
            collective_id=0, has_side_effects=True, vmem_limit_bytes=60 * 2**20
        ),
    )(queries, key_rows, value_rows, attn_out, log_norm.T, grad_out, block_pos)


def solution(mesh):
    split = P("ctx", "tp")
    joint = P(("ctx", "tp"), None)
    return jax.shard_map(
        per_device,
        mesh=mesh,
        in_specs=(split, split, split, split, split, joint, P()),
        out_specs=(joint, joint, joint),
        check_vma=False,
    )
```

time: 77.8 us -> 67.3 us (0.87)
  Pallas kernels: 71.3 us -> 63.4 us
  local copies, waits for them, and re-layouts: 5.6 us -> 3.06 us
    pallas_call x1, Pallas kernels: 71.3 us -> 63.4 us  [per_device(): pl.pallas_call(kernel, out_shape=[jax.ShapeDtypeStruct((piece, NT * ROWS)...]
    unnamed x16 -> x7, local copies, waits for them, and re-layouts: 5.6 us -> 3.06 us
where the time goes in v2:
time: 67.3 us; the launch traced here: 67.1 us
  Pallas kernels  63.4 us (94%)
  local copies, waits for them, and re-layouts  3.06 us (5%)
    pallas_call x1, Pallas kernels, per_device(): pl.pallas_call(kernel, out_shape=[jax.ShapeDtypeStruct((piece, NT * ROWS)...  63.4 us
    unnamed x7, local copies, waits for them, and re-layouts  3.06 us

profile of v2, /device:TPU:1, one launch (start us, length us, event | category | flops | bytes accessed | tf_op | source)
XLA Modules:
  0.0 67.1 jit_solution(5015134313152730384)
XLA Ops:
  0.6 63.4 %shard_map.94 = (bf16[32,4096]{1,0:T(8,128)(2,1)}, bf16[32,512]{1,0:T(8,128)(2,1)}, bf16[32,512]{1,0:T(8,128)(2,1)}) custom-call(bf16[128,1024]{1,0:T(8,128)(2,1)} %q_hbm.1, bf16[128,128]{1,0:T(8,128)(2,1)} %k_in.1, bf16[128,128]{1,0:T(8,128)(2,1)} %v_in.1, bf16[128,1024]{1,0:T(8,128)(2,1)} %o_hbm.1, f32[8,128]{1,0:T(8,128)} %bitcast.1, ...), custom_call_target="tpu_custom_call" | custom-call | tf_op jit(solution)/shard_map/pallas_call | solution.py:413
  64.0 0.0 copy-start.1
  64.0 1.7 %copy.13 = bf16[32,4096]{1,0:T(8,128)(2,1)} copy(bf16[32,4096]{1,0:T(8,128)(2,1)} %get-tuple-element.6) | data formatting | bytes 524288
  65.7 0.0 copy-done.1
  65.7 0.0 copy-start
  65.7 0.6 copy.14
  66.3 0.2 copy-done
  66.5 0.6 copy.15
Async XLA Ops:
  64.0 1.7 %copy-start.1 = (bf16[32,512]{1,0:T(8,128)(2,1)S(1)}, bf16[32,512]{1,0:T(8,128)(2,1)}, u32[]{:S(2)}) copy-start(bf16[32,512]{1,0:T(8,128)(2,1)} %get-tuple-element.7) | copy-start | bytes 98308
  65.7 0.8 %copy-start = (bf16[32,512]{1,0:T(8,128)(2,1)S(1)}, bf16[32,512]{1,0:T(8,128)(2,1)}, u32[]{:S(2)}) copy-start(bf16[32,512]{1,0:T(8,128)(2,1)} %get-tuple-element.8) | copy-start | bytes 98308

commit v3 on v2

--- a/solution.py
+++ b/solution.py
@@ -77,6 +77,8 @@
     peers = [group_dev(dx, dt) for dx, dt in group]
     peers += [dev(xl, z, lax.rem(y + dy, NY), t) for dy in range(1, NY)]
     peers += [dev(xl, lax.rem(z + dz, NZ), y, t) for dz in range(1, NZ)]
+    next_rows = sorted({1, NZ - 1})
+    peers += [dev(xl, lax.rem(z + dz, NZ), lax.rem(y + dy, NY), t) for dz in next_rows for dy in range(1, NY)]
     for peer in peers:
         pl.semaphore_signal(barrier, inc=1, device_id=peer, device_id_type=MESH)
 
@@ -131,6 +133,14 @@
     def ld_copy():
         return copy(ld.at[0], ld.at[1], ld_s.at[0], ld_r.at[0], dev(xp, z, y, t))
 
+    def next_keys(dz, dy):
+        to = dev(xl, lax.rem(z + dz, NZ), lax.rem(y + dy, NY), t)
+        return copy(kk.at[z, 0], kk.at[z, dy], ring_s.at[0], ring_r.at[0], to)
+
+    def next_values(dz, dy):
+        to = dev(xl, lax.rem(z + dz, NZ), lax.rem(y + dy, NY), t)
+        return copy(vv.at[z, 0], vv.at[z, dy], vy_s.at[0], vy_r.at[z], to)
+
     def ring_copy(step, back):
         row = lax.rem(z + step, NZ) if back else wrap(z - step, NZ)
         to = wrap(z - 1, NZ) if back else lax.rem(z + 1, NZ)
@@ -170,8 +180,13 @@
     near_first = [dz for _, dz in sorted((min(dz, NZ - dz), dz) for dz in range(1, NZ))]
     for dy in range(1, NY):
         vy_copy(z, dy).start()
-    for dz in near_first[:2]:
+    for dz in next_rows:
+        for dy in range(NY):
+            next_keys(dz, dy).start()
+    for dz in next_rows:
         vz_copy(dz).start()
+        for dy in range(1, NY):
+            next_values(dz, dy).start()
 
     sub16 = lax.broadcasted_iota(jnp.int32, (16, TOK), 0)
     tok16 = lax.broadcasted_iota(jnp.int32, (16, TOK), 1)
@@ -221,19 +236,18 @@
     for dt in range(NT):
         do_copy(1, dt).start()
     q_copy().start()
-    for dz in near_first[2:]:
+    for dz in near_first[len(next_rows):]:
         vz_copy(dz).start()
 
     settle(kk.at[z, 1:], ky_r.at[0])
-    ring_copy(0, 0).start()
-    ring_copy(0, 1).start()
 
     def pass_values(dist):
         both = sorted({dist, NZ - dist})
         settle(vv.at[:len(both), 0], vz_r.at[dist])
         for dz in both:
-            for dy in range(1, NY):
-                vy_copy(wrap(z - dz, NZ), dy).start()
+            if dist > 1:
+                for dy in range(1, NY):
+                    vy_copy(wrap(z - dz, NZ), dy).start()
 
     def pass_keys(dist):
         settle(kk.at[:2 if dist < NZ // 2 else 1], ring_r.at[dist - 1])

time: 67.3 us -> 65 us (0.966)
  Pallas kernels: 63.4 us -> 61.1 us
    pallas_call x1, Pallas kernels: 63.4 us -> 61.1 us  [per_device(): pl.pallas_call(kernel, out_shape=[jax.ShapeDtypeStruct((piece, NT * ROWS)...]
where the time goes in v3:
time: 65 us; the launch traced here: 64.8 us
  Pallas kernels  61.1 us (94%)
  local copies, waits for them, and re-layouts  3.06 us (5%)
  between operations  0.65 us (1%)
    pallas_call x1, Pallas kernels, per_device(): pl.pallas_call(kernel, out_shape=[jax.ShapeDtypeStruct((piece, NT * ROWS)...  61.1 us
    unnamed x7, local copies, waits for them, and re-layouts  3.06 us

profile of v3, /device:TPU:1, one launch (start us, length us, event | category | flops | bytes accessed | tf_op | source)
XLA Modules:
  0.0 64.8 jit_solution(11398453984418622454)
XLA Ops:
  0.6 61.1 %shard_map.94 = (bf16[32,4096]{1,0:T(8,128)(2,1)}, bf16[32,512]{1,0:T(8,128)(2,1)}, bf16[32,512]{1,0:T(8,128)(2,1)}) custom-call(bf16[128,1024]{1,0:T(8,128)(2,1)} %q_hbm.1, bf16[128,128]{1,0:T(8,128)(2,1)} %k_in.1, bf16[128,128]{1,0:T(8,128)(2,1)} %v_in.1, bf16[128,1024]{1,0:T(8,128)(2,1)} %o_hbm.1, f32[8,128]{1,0:T(8,128)} %bitcast.1, ...), custom_call_target="tpu_custom_call" | custom-call | tf_op jit(solution)/shard_map/pallas_call | solution.py:427
  61.7 0.0 copy-start.1
  61.7 1.7 %copy.13 = bf16[32,4096]{1,0:T(8,128)(2,1)} copy(bf16[32,4096]{1,0:T(8,128)(2,1)} %get-tuple-element.6) | data formatting | bytes 524288
  63.4 0.0 copy-done.1
  63.4 0.0 copy-start
  63.4 0.6 copy.14
  64.0 0.2 copy-done
  64.2 0.6 copy.15
Async XLA Ops:
  61.7 1.7 %copy-start.1 = (bf16[32,512]{1,0:T(8,128)(2,1)S(1)}, bf16[32,512]{1,0:T(8,128)(2,1)}, u32[]{:S(2)}) copy-start(bf16[32,512]{1,0:T(8,128)(2,1)} %get-tuple-element.7) | copy-start | bytes 98308
  63.4 0.8 %copy-start = (bf16[32,512]{1,0:T(8,128)(2,1)S(1)}, bf16[32,512]{1,0:T(8,128)(2,1)}, u32[]{:S(2)}) copy-start(bf16[32,512]{1,0:T(8,128)(2,1)} %get-tuple-element.8) | copy-start | bytes 98308

commit v4 on v3

--- a/solution.py
+++ b/solution.py
@@ -79,8 +79,6 @@
     peers += [dev(xl, lax.rem(z + dz, NZ), y, t) for dz in range(1, NZ)]
     next_rows = sorted({1, NZ - 1})
     peers += [dev(xl, lax.rem(z + dz, NZ), lax.rem(y + dy, NY), t) for dz in next_rows for dy in range(1, NY)]
-    for peer in peers:
-        pl.semaphore_signal(barrier, inc=1, device_id=peer, device_id_type=MESH)
 
     fetches = [
         pltpu.make_async_copy(src, dst, loc.at[at])
@@ -99,6 +97,8 @@
     ]
     for fetch in fetches:
         fetch.start()
+    for peer in peers:
+        pl.semaphore_signal(barrier, inc=1, device_id=peer, device_id_type=MESH)
     pl.semaphore_wait(barrier, len(peers))
 
     def copy(src, dst, send, recv, device):

time: 65 us -> 65 us (level)
  no operation moved by 1% of the time
where the time goes in v4:
time: 65 us; the launch traced here: 64.9 us
  Pallas kernels  61.1 us (94%)
  local copies, waits for them, and re-layouts  3.06 us (5%)
  between operations  0.65 us (1%)
    pallas_call x1, Pallas kernels, per_device(): pl.pallas_call(kernel, out_shape=[jax.ShapeDtypeStruct((piece, NT * ROWS)...  61.1 us
    unnamed x7, local copies, waits for them, and re-layouts  3.06 us

profile of v4, /device:TPU:1, one launch (start us, length us, event | category | flops | bytes accessed | tf_op | source)
XLA Modules:
  0.0 64.9 jit_solution(326937161037541168)
XLA Ops:
  0.6 61.1 %shard_map.94 = (bf16[32,4096]{1,0:T(8,128)(2,1)}, bf16[32,512]{1,0:T(8,128)(2,1)}, bf16[32,512]{1,0:T(8,128)(2,1)}) custom-call(bf16[128,1024]{1,0:T(8,128)(2,1)} %q_hbm.1, bf16[128,128]{1,0:T(8,128)(2,1)} %k_in.1, bf16[128,128]{1,0:T(8,128)(2,1)} %v_in.1, bf16[128,1024]{1,0:T(8,128)(2,1)} %o_hbm.1, f32[8,128]{1,0:T(8,128)} %bitcast.1, ...), custom_call_target="tpu_custom_call" | custom-call | tf_op jit(solution)/shard_map/pallas_call | solution.py:427
  61.8 0.0 copy-start.1
  61.8 1.7 %copy.13 = bf16[32,4096]{1,0:T(8,128)(2,1)} copy(bf16[32,4096]{1,0:T(8,128)(2,1)} %get-tuple-element.6) | data formatting | bytes 524288
  63.5 0.0 copy-done.1
  63.5 0.0 copy-start
  63.5 0.6 copy.14
  64.1 0.2 copy-done
  64.2 0.6 copy.15
Async XLA Ops:
  61.8 1.7 %copy-start.1 = (bf16[32,512]{1,0:T(8,128)(2,1)S(1)}, bf16[32,512]{1,0:T(8,128)(2,1)}, u32[]{:S(2)}) copy-start(bf16[32,512]{1,0:T(8,128)(2,1)} %get-tuple-element.7) | copy-start | bytes 98308
  63.5 0.8 %copy-start = (bf16[32,512]{1,0:T(8,128)(2,1)S(1)}, bf16[32,512]{1,0:T(8,128)(2,1)}, u32[]{:S(2)}) copy-start(bf16[32,512]{1,0:T(8,128)(2,1)} %get-tuple-element.8) | copy-start | bytes 98308
